TPU v7x, 512 devices: a whole 4x4x16 slice. The times are simulated.
512 devices in a mesh: gx: 32 (over z, core), gy: 16 (over x, y).
Axes of the slice: x: 4, y: 4, z: 16, core: 2. Of those that a mesh axis runs over, the one named last changes fastest.
Arguments:
- adjoint: float32 [3, 8, 512, 2048], P(None, None, 'gx', 'gy'), may hold values from -12 to 12
- checkpoints: bfloat16 [1, 3, 8, 512, 2048], P(None, None, None, 'gx', 'gy'), may hold values from -3 to 3
- wall_faces: int32 [2, 64, 256], P(None, 'gx', 'gy'), may hold values 0 or 1
Outputs:
- velocity: float32 [3, 8, 512, 2048], P(None, None, 'gx', 'gy')
- pressure: float32 [8, 512, 2048], P(None, 'gx', 'gy')
Inputs may be any that keep to these rules, and one draw needn't show every extreme that they name: `wall_faces`: 1 marks a no-slip face, 0 an open one.
All inputs are finite; a program needn't handle non-finite values. No bound on the sum of `wall_faces` on one device may be relied on, other than what follows from the above.
Results may differ from a plain program's by a relative error of at most 0.0003.
Values sent between devices are 32-bit elements; how exact they have to be, the bound alone decides.
No kernel may reach another device: no remote copies, remote signals or barrier semaphores. Data moves between devices by JAX's collectives and lax.ppermute only.
A program may use at most 64 MiB of HBM per device.

v0:
```python
import jax
import jax.numpy as jnp
import numpy as np
from jax import lax
from jax.sharding import PartitionSpec as P

ITERS = 4
node_points = np.array(
    [
        -1.0,
        -0.8717401485096066,
        -0.5917001814331423,
        -0.2092992179024789,
        0.2092992179024789,
        0.5917001814331423,
        0.8717401485096066,
        1.0,
    ]
)
node_weights = np.array(
    [
        0.03571428571428571,
        0.2107042271435061,
        0.3411226924835044,
        0.4124587946587038,
        0.4124587946587038,
        0.3411226924835044,
        0.2107042271435061,
        0.03571428571428571,
    ]
)
time_step = 0.05
viscosity = 0.02
highest = lax.Precision.HIGHEST


def with_halo(value, sides, width):
    for axis, dim in sides:
        size, length = (lax.axis_size(axis), value.shape[dim])
        up = [(i, (i + 1) % size) for i in range(size)]
        down = [(j, i) for i, j in up]
        last = lax.slice_in_dim(value, length - width, length, axis=dim)
        initial = lax.slice_in_dim(value, 0, width, axis=dim)
        before = lax.ppermute(last, axis, up)
        after = lax.ppermute(initial, axis, down)
        value = jnp.concatenate([before, value, after], axis=dim)
    return value


def derivative_table(points):
    identity = np.eye(points.shape[0])
    spacing = points[:, None] - points[None, :] + identity
    barycentric = 1.0 / np.prod(spacing, axis=1)
    matrix = barycentric[None, :] / barycentric[:, None] / spacing
    matrix = matrix * (1.0 - identity)
    return matrix - identity * np.sum(matrix, axis=1)[:, None]


def along_rows(nodal, matrix):
    blocked = jnp.asarray(np.kron(np.eye(nodal.shape[2] // 8), matrix), jnp.float32)
    return jnp.einsum("xk,czky->czxy", blocked, nodal, precision=highest)


def along_columns(nodal, matrix):
    size_y = nodal.shape[3]
    block_width = 128 if size_y % 128 == 0 else size_y
    blocked = jnp.asarray(np.kron(np.eye(block_width // 8), matrix).T, jnp.float32)
    grouped = nodal.reshape(
        nodal.shape[0], nodal.shape[1], nodal.shape[2], size_y // block_width, block_width
    )
    result = jnp.einsum("czxgk,kb->czxgb", grouped, blocked, precision=highest)
    return result.reshape(nodal.shape)


def along_depth(nodal, matrix):
    return jnp.einsum("ck,akxy->acxy", jnp.asarray(matrix, jnp.float32), nodal, precision=highest)


def mass_weights(size_x, size_y):
    weights = jnp.asarray(node_weights, jnp.float32)
    across_x = jnp.tile(weights, size_x // 8)
    across_y = jnp.tile(weights, size_y // 8)
    return weights[:, None, None] * across_x[None, :, None] * across_y[None, None, :]


def edge_flags(length):
    place = jnp.arange(length) % 8
    return ((place == 0) | (place == 7)).astype(jnp.float32)


def share_counts(size_x, size_y):
    return (1.0 + edge_flags(size_x))[:, None] * (1.0 + edge_flags(size_y))[None, :]


def boundary_masks(wall_faces, size_x, size_y):
    walls = jnp.repeat(jnp.repeat(wall_faces.astype(jnp.float32), 8, axis=1), 8, axis=2)
    interior = (1.0 - edge_flags(size_x))[:, None] * (1.0 - edge_flags(size_y))[None, :]
    middle = jnp.ones((6, size_x, size_y), jnp.float32)
    velocity_mask = jnp.concatenate(
        [(interior * (1.0 - walls[0]))[None], middle, (interior * (1.0 - walls[1]))[None]], axis=0
    )
    pressure_mask = jnp.concatenate(
        [(interior * walls[0])[None], middle, (interior * walls[1])[None]], axis=0
    )
    return (velocity_mask, pressure_mask)


def sum_rows(padded):
    size_x = padded.shape[2] - 2
    place = jnp.arange(size_x) % 8
    upper = (place == 7).astype(jnp.float32)[:, None]
    lower = (place == 0).astype(jnp.float32)[:, None]
    return padded[:, :, 1:-1, :] + upper * padded[:, :, 2:, :] + lower * padded[:, :, :-2, :]


def sum_columns(padded):
    size_y = padded.shape[3] - 2
    place = jnp.arange(size_y) % 8
    upper = (place == 7).astype(jnp.float32)
    lower = (place == 0).astype(jnp.float32)
    return padded[:, :, :, 1:-1] + upper * padded[:, :, :, 2:] + lower * padded[:, :, :, :-2]


def assemble_velocity(nodal):
    padded = with_halo(nodal, (("gx", 2), ("gy", 3)), 1)
    return sum_columns(sum_rows(padded))


def assemble_pressure(nodal):
    padded = with_halo(nodal, (("gx", 2), ("gy", 3)), 1)
    return sum_columns(sum_rows(padded))


def stiffness(nodal, wmass):
    derivative = derivative_table(node_points)
    transposed = derivative.T
    return (
        along_rows(wmass * along_rows(nodal, derivative), transposed)
        + along_columns(wmass * along_columns(nodal, derivative), transposed)
        + along_depth(wmass * along_depth(nodal, derivative), transposed)
    )


def inner(former, latter, inverse_share):
    return jnp.sum(former * latter * inverse_share)


def solve_pressure(source, pressure_mask, wmass, inverse_share):
    pressure = jnp.zeros_like(source)
    resid = source
    direction = source
    norm_now = jnp.zeros((), jnp.float32)
    for round_index in range(ITERS):
        image = pressure_mask * assemble_pressure(stiffness(direction, wmass))
        if round_index == 0:
            norm_now, curve = lax.psum(
                (inner(resid, resid, inverse_share), inner(direction, image, inverse_share)),
                ("gx", "gy"),
            )
        else:
            curve = lax.psum(inner(direction, image, inverse_share), ("gx", "gy"))
        step_length = norm_now / curve
        pressure = pressure + step_length * direction
        resid = resid - step_length * image
        if round_index + 1 < ITERS:
            norm_next = lax.psum(inner(resid, resid, inverse_share), ("gx", "gy"))
            direction = resid + norm_next / norm_now * direction
            norm_now = norm_next
    return pressure


def adjoint_step(velocity, forward, velocity_mask, pressure_mask, wmass, amass, inverse_share):
    derivative = derivative_table(node_points)
    flow = forward.astype(jnp.float32)
    flow_dx = along_rows(flow, derivative)
    flow_dy = along_columns(flow, derivative)
    flow_dz = along_depth(flow, derivative)
    velocity_dx = along_rows(velocity, derivative)
    velocity_dy = along_columns(velocity, derivative)
    velocity_dz = along_depth(velocity, derivative)
    transport = flow[0:1] * velocity_dx + flow[1:2] * velocity_dy + flow[2:3] * velocity_dz
    stretch = jnp.concatenate(
        [
            jnp.sum(velocity * flow_dx, axis=0, keepdims=True),
            jnp.sum(velocity * flow_dy, axis=0, keepdims=True),
            jnp.sum(velocity * flow_dz, axis=0, keepdims=True),
        ],
        axis=0,
    )
    advect = transport - stretch
    forcing = wmass * (velocity + time_step * advect) - time_step * viscosity * stiffness(
        velocity, wmass
    )
    moved = velocity_mask * assemble_velocity(forcing) / amass
    diverge = (
        along_rows(moved[0:1], derivative)
        + along_columns(moved[1:2], derivative)
        + along_depth(moved[2:3], derivative)
    )
    source = -pressure_mask * assemble_pressure(wmass * diverge)
    pressure = solve_pressure(source, pressure_mask, wmass, inverse_share)
    slopes = jnp.concatenate(
        [
            along_rows(pressure, derivative),
            along_columns(pressure, derivative),
            along_depth(pressure, derivative),
        ],
        axis=0,
    )
    correction = assemble_velocity(wmass * slopes) / amass
    return (velocity_mask * (moved - correction), pressure)


def local(adjoint, checkpoints, wall_faces):
    size_x = adjoint.shape[2]
    size_y = adjoint.shape[3]
    wmass = mass_weights(size_x, size_y)
    counts = share_counts(size_x, size_y)
    inverse_share = 1.0 / counts
    amass = wmass * counts
    velocity_mask, pressure_mask = boundary_masks(wall_faces, size_x, size_y)
    velocity = adjoint
    velocity, pressure = adjoint_step(
        velocity, checkpoints[0], velocity_mask, pressure_mask, wmass, amass, inverse_share
    )
    return (velocity, pressure[0])


def solution(mesh):
    return jax.shard_map(
        local,
        mesh=mesh,
        in_specs=(P(None, None, "gx", "gy"), P(None, None, None, "gx", "gy"), P(None, "gx", "gy")),
        out_specs=(P(None, None, "gx", "gy"), P(None, "gx", "gy")),
        check_vma=False,
    )
```

profile of v0, /device:TPU:1, one launch (start us, length us, event | category | flops | bytes accessed | tf_op | source)
XLA Modules:
  0.0 876.8 jit_solution(5244411411854615604)
XLA Ops:
  0.7 0.7 copy-done.11
  1.3 1.3 convolution_bitcast_fusion.3
  4.1 0.6 copy-done.15
  6.4 0.7 copy-done.13
  9.0 3.0 collective-permute-start
  12.1 3.9 collective-permute-start.1
  17.0 1.9 collective-permute-start.2
  18.9 6.7 collective-permute-start.3
  25.6 2.2 collective-permute-done.2
  27.8 1.5 collective-permute-done.3
  30.0 0.8 copy-done.1
  32.4 1.8 collective-permute-start.4
  34.3 3.5 collective-permute-start.5
  37.8 0.6 collective-permute-done.4
  38.7 1.9 collective-permute-start.6
  40.6 7.4 collective-permute-start.7
  48.1 1.6 collective-permute-done.7
  50.9 0.7 copy-done.3
  53.3 6.4 collective-permute-start.9
  59.7 0.6 collective-permute-done.8
  60.6 1.9 collective-permute-start.10
  62.6 7.4 collective-permute-start.11
  70.0 1.6 collective-permute-done.11
  71.8 0.8 multiply_reduce_fusion.5
  72.6 108.5 %all-reduce = (f32[]{:T(128)}, f32[]{:T(128)}) all-reduce(f32[]{:T(128)} %get-tuple-element.3, f32[]{:T(128)} %get-tuple-element.2), channel_id=1, replica_groups=mesh['gx'=32,'gy'=16] {'gx','gy'}, use_global_device_ids=true, to_apply=%region_4.5 | all-reduce | flops 2 | bytes 16 | tf_op jit(solution)/shard_map/psum | solution.py:156
  182.5 0.7 multiply_reduce_fusion.4
  183.2 98.5 %psum.58 = f32[]{:T(128)} all-reduce(f32[]{:T(128)} %multiply_reduce_fusion.4), channel_id=1, replica_groups=mesh['gx'=32,'gy'=16] {'gx','gy'}, use_global_device_ids=true, to_apply=%region_8.9 | all-reduce | flops 1 | bytes 8 | tf_op jit(solution)/shard_map/psum | solution.py:166
  284.5 2.3 collective-permute-start.12
  286.8 0.8 collective-permute-done.12
  287.6 2.3 collective-permute-done.13
  289.9 2.2 collective-permute-start.14
  292.2 6.4 collective-permute-start.15
  298.6 1.4 collective-permute-done.14
  299.9 0.9 collective-permute-done.15
  301.1 0.7 multiply_reduce_fusion.3
  301.8 102.7 %psum.59 = f32[]{:T(128)} all-reduce(f32[]{:T(128)} %get-tuple-element.10), channel_id=1, replica_groups=mesh['gx'=32,'gy'=16] {'gx','gy'}, use_global_device_ids=true, to_apply=%region_10.11 | all-reduce | flops 1 | bytes 8 | tf_op jit(solution)/shard_map/psum | solution.py:161
  405.9 0.7 multiply_reduce_fusion.2
  406.6 99.3 %psum.60 = f32[]{:T(128)} all-reduce(f32[]{:T(128)} %get-tuple-element.8), channel_id=1, replica_groups=mesh['gx'=32,'gy'=16] {'gx','gy'}, use_global_device_ids=true, to_apply=%region_12.13 | all-reduce | flops 1 | bytes 8 | tf_op jit(solution)/shard_map/psum | solution.py:166
  508.6 1.4 collective-permute-start.16
  510.1 0.8 collective-permute-done.16
  510.8 2.3 collective-permute-done.17
  513.3 2.3 collective-permute-start.18
  515.6 6.3 collective-permute-start.19
  522.4 1.1 collective-permute-done.19
  523.8 0.7 multiply_reduce_fusion.1
  524.5 104.3 %psum.61 = f32[]{:T(128)} all-reduce(f32[]{:T(128)} %get-tuple-element.6), channel_id=1, replica_groups=mesh['gx'=32,'gy'=16] {'gx','gy'}, use_global_device_ids=true, to_apply=%region_14.15 | all-reduce | flops 1 | bytes 8 | tf_op jit(solution)/shard_map/psum | solution.py:161
  630.8 98.4 %psum.62 = f32[]{:T(128)} all-reduce(f32[]{:T(128)} %multiply_reduce_fusion), channel_id=1, replica_groups=mesh['gx'=32,'gy'=16] {'gx','gy'}, use_global_device_ids=true, to_apply=%region_16.17 | all-reduce | flops 1 | bytes 8 | tf_op jit(solution)/shard_map/psum | solution.py:166
  731.9 2.3 collective-permute-start.20
  734.3 0.8 collective-permute-done.20
  735.0 2.3 collective-permute-done.21
  737.4 2.5 collective-permute-start.22
  739.9 6.1 collective-permute-start.23
  746.0 1.4 collective-permute-done.22
  747.4 0.9 collective-permute-done.23
  748.6 0.7 fusion.73
  749.3 102.6 %psum.63 = f32[]{:T(128)} all-reduce(f32[]{:T(128)} %fusion.73), channel_id=1, replica_groups=mesh['gx'=32,'gy'=16] {'gx','gy'}, use_global_device_ids=true, to_apply=%region_18.19 | all-reduce | flops 1 | bytes 8 | tf_op jit(solution)/shard_map/psum | solution.py:161
  854.3 2.7 collective-permute-start.24
  857.0 0.8 collective-permute-done.24
  857.8 2.3 collective-permute-done.25
  860.3 1.9 collective-permute-start.26
  862.2 6.7 collective-permute-start.27
  868.9 5.4 collective-permute-done.26
  874.3 1.0 collective-permute-done.27
  875.8 1.0 fusion.35
  (159 shorter events, 20.0 us)
Async XLA Ops:
  0.6 0.7 copy-start.11
  1.3 1.3 copy-start
  1.3 1.3 copy-start.2
  2.7 0.8 copy-start.6
  4.1 0.7 copy-start.15
  4.9 0.7 copy-start.12
  6.4 0.7 copy-start.13
  7.1 0.7 copy-start.14
  7.7 0.8 copy-start.10
  9.0 7.6 collective-permute-start
  12.1 3.9 copy-start.16
  12.1 4.7 collective-permute-start.1
  17.0 10.8 %collective-permute-start.2 = (f32[3,8,18,1]{3,2,1,0:T(8,128)S(1)}, f32[3,8,18,1]{3,2,1,0:T(8,128)S(1)}, u32[]{:S(2)}, u32[]{:S(2)}) collective-permute-start(f32[3,8,18,1]{3,2,1,0:T(8,128)S(1)} %get-tuple-element.15), channel_id=1, source_target_pairs={{0,1},{1,2},{2,3},{3,4},{4,5},{5,6},{6,7},{7,8},{8,9},{9,10},{10,1... | collective-permute-start | bytes 5192 | tf_op jit(solution)/shard_map/ppermute | solution.py:44
  18.9 10.3 %collective-permute-start.3 = (f32[3,8,18,1]{3,2,1,0:T(8,128)S(1)}, f32[3,8,18,1]{3,2,1,0:T(8,128)S(1)}, u32[]{:S(2)}, u32[]{:S(2)}) collective-permute-start(f32[3,8,18,1]{3,2,1,0:T(8,128)S(1)} %get-tuple-element.16), channel_id=1, source_target_pairs={{1,0},{2,1},{3,2},{4,3},{5,4},{6,5},{7,6},{8,7},{9,8},{10,9},{11,1... | collective-permute-start | bytes 5192 | tf_op jit(solution)/shard_map/ppermute | solution.py:45
  30.0 0.8 copy-start.1
  30.8 0.7 copy-start.7
  31.5 0.7 copy-start.5
  32.4 5.9 collective-permute-start.4
  34.3 4.3 collective-permute-start.5
  38.7 9.4 %collective-permute-start.6 = (f32[1,8,18,1]{3,2,1,0:T(8,128)S(1)}, f32[1,8,18,1]{3,2,1,0:T(8,128)S(1)}, u32[]{:S(2)}, u32[]{:S(2)}) collective-permute-start(f32[1,8,18,1]{3,2,1,0:T(8,128)S(1)} %get-tuple-element.32), channel_id=1, source_target_pairs={{0,1},{1,2},{2,3},{3,4},{4,5},{5,6},{6,7},{7,8},{8,9},{9,10},{10,1... | collective-permute-start | bytes 1736 | tf_op jit(solution)/shard_map/ppermute | solution.py:44
  40.6 9.1 %collective-permute-start.7 = (f32[1,8,18,1]{3,2,1,0:T(8,128)S(1)}, f32[1,8,18,1]{3,2,1,0:T(8,128)S(1)}, u32[]{:S(2)}, u32[]{:S(2)}) collective-permute-start(f32[1,8,18,1]{3,2,1,0:T(8,128)S(1)} %get-tuple-element.33), channel_id=1, source_target_pairs={{1,0},{2,1},{3,2},{4,3},{5,4},{6,5},{7,6},{8,7},{9,8},{10,9},{11,1... | collective-permute-start | bytes 1736 | tf_op jit(solution)/shard_map/ppermute | solution.py:45
  50.8 0.8 copy-start.3
  51.6 0.7 copy-start.9
  52.3 0.7 copy-start.8
  53.3 7.1 collective-permute-start.8
  53.3 7.3 collective-permute-start.9
  60.6 9.4 %collective-permute-start.10 = (f32[1,8,18,1]{3,2,1,0:T(8,128)S(1)}, f32[1,8,18,1]{3,2,1,0:T(8,128)S(1)}, u32[]{:S(2)}, u32[]{:S(2)}) collective-permute-start(f32[1,8,18,1]{3,2,1,0:T(8,128)S(1)} %get-tuple-element.30), channel_id=1, source_target_pairs={{0,1},{1,2},{2,3},{3,4},{4,5},{5,6},{6,7},{7,8},{8,9},{9,10},{10,1... | collective-permute-start | bytes 1736 | tf_op jit(solution)/shard_map/ppermute | solution.py:44
  62.6 9.0 %collective-permute-start.11 = (f32[1,8,18,1]{3,2,1,0:T(8,128)S(1)}, f32[1,8,18,1]{3,2,1,0:T(8,128)S(1)}, u32[]{:S(2)}, u32[]{:S(2)}) collective-permute-start(f32[1,8,18,1]{3,2,1,0:T(8,128)S(1)} %get-tuple-element.31), channel_id=1, source_target_pairs={{1,0},{2,1},{3,2},{4,3},{5,4},{6,5},{7,6},{8,7},{9,8},{10,9},{11,1... | collective-permute-start | bytes 1736 | tf_op jit(solution)/shard_map/ppermute | solution.py:45
  284.5 3.1 collective-permute-start.12
  286.8 3.0 collective-permute-start.13
  289.9 10.0 %collective-permute-start.14 = (f32[1,8,18,1]{3,2,1,0:T(8,128)S(1)}, f32[1,8,18,1]{3,2,1,0:T(8,128)S(1)}, u32[]{:S(2)}, u32[]{:S(2)}) collective-permute-start(f32[1,8,18,1]{3,2,1,0:T(8,128)S(1)} %get-tuple-element.28), channel_id=1, source_target_pairs={{0,1},{1,2},{2,3},{3,4},{4,5},{5,6},{6,7},{7,8},{8,9},{9,10},{10,1... | collective-permute-start | bytes 1736 | tf_op jit(solution)/shard_map/ppermute | solution.py:44
  292.2 8.7 collective-permute-start.15
  508.6 2.2 collective-permute-start.16
  510.1 3.1 collective-permute-start.17
  513.3 9.1 %collective-permute-start.18 = (f32[1,8,18,1]{3,2,1,0:T(8,128)S(1)}, f32[1,8,18,1]{3,2,1,0:T(8,128)S(1)}, u32[]{:S(2)}, u32[]{:S(2)}) collective-permute-start(f32[1,8,18,1]{3,2,1,0:T(8,128)S(1)} %get-tuple-element.26), channel_id=1, source_target_pairs={{0,1},{1,2},{2,3},{3,4},{4,5},{5,6},{6,7},{7,8},{8,9},{9,10},{10,1... | collective-permute-start | bytes 1736 | tf_op jit(solution)/shard_map/ppermute | solution.py:44
  515.6 7.9 collective-permute-start.19
  731.9 3.1 collective-permute-start.20
  734.3 3.0 collective-permute-start.21
  737.4 10.0 %collective-permute-start.22 = (f32[1,8,18,1]{3,2,1,0:T(8,128)S(1)}, f32[1,8,18,1]{3,2,1,0:T(8,128)S(1)}, u32[]{:S(2)}, u32[]{:S(2)}) collective-permute-start(f32[1,8,18,1]{3,2,1,0:T(8,128)S(1)} %get-tuple-element.24), channel_id=1, source_target_pairs={{0,1},{1,2},{2,3},{3,4},{4,5},{5,6},{6,7},{7,8},{8,9},{9,10},{10,1... | collective-permute-start | bytes 1736 | tf_op jit(solution)/shard_map/ppermute | solution.py:44
  739.9 8.4 collective-permute-start.23
  853.4 0.6 copy-start.4
  854.3 3.5 collective-permute-start.24
  857.0 3.1 collective-permute-start.25
  860.3 14.0 %collective-permute-start.26 = (f32[3,8,18,1]{3,2,1,0:T(8,128)S(1)}, f32[3,8,18,1]{3,2,1,0:T(8,128)S(1)}, u32[]{:S(2)}, u32[]{:S(2)}) collective-permute-start(f32[3,8,18,1]{3,2,1,0:T(8,128)S(1)} %get-tuple-element.13), channel_id=1, source_target_pairs={{0,1},{1,2},{2,3},{3,4},{4,5},{5,6},{6,7},{7,8},{8,9},{9,10},{10,1... | collective-permute-start | bytes 5192 | tf_op jit(solution)/shard_map/ppermute | solution.py:44
  862.2 13.1 %collective-permute-start.27 = (f32[3,8,18,1]{3,2,1,0:T(8,128)S(1)}, f32[3,8,18,1]{3,2,1,0:T(8,128)S(1)}, u32[]{:S(2)}, u32[]{:S(2)}) collective-permute-start(f32[3,8,18,1]{3,2,1,0:T(8,128)S(1)} %get-tuple-element.14), channel_id=1, source_target_pairs={{1,0},{2,1},{3,2},{4,3},{5,4},{6,5},{7,6},{8,7},{9,8},{10,9},{11,1... | collective-permute-start | bytes 5192 | tf_op jit(solution)/shard_map/ppermute | solution.py:45
where the time goes:
time: 879 us; the launch traced here: 877 us
  blocking collectives  714 us (81%)
  starting transfers between devices  89.1 us (10%)
  waiting for transfers between devices  33.5 us (4%)
  between operations  10.9 us (1%)
  other arithmetic  10 us (1%)
  matrix products  9.55 us (1%)
  local copies, waits for them, and re-layouts  9.23 us (1%)
    psum x3, blocking collectives, solve_pressure(): curve = lax.psum(inner(direction, image, inverse_share), ('gx', 'gy'))  310 us
    psum x3, blocking collectives, solve_pressure(): norm_next = lax.psum(inner(resid, resid, inverse_share), ('gx', 'gy'))  296 us
    psum x1, blocking collectives, solve_pressure(): lax.psum((inner(resid, resid, inverse_share), inner(direction, image, inv...  109 us
    ppermute x14, starting transfers between devices, with_halo(): after = lax.ppermute(initial, axis, down)  60.8 us
    ppermute x14, starting transfers between devices, with_halo(): before = lax.ppermute(last, axis, up)  28.4 us
    ppermute x14, waiting for transfers between devices, with_halo(): after = lax.ppermute(initial, axis, down)  18.2 us
  transfers between devices with their start and end apart: 28, of which 27 were waited for; matrix products, arithmetic and copies ran while one was open for 0% of the time, Pallas kernels for 0%

commit v1 on v0

--- a/solution.py
+++ b/solution.py
@@ -158,7 +158,7 @@
                 ("gx", "gy"),
             )
         else:
-            curve = lax.psum(inner(direction, image, inverse_share), ("gx", "gy"))
+            curve = lax.psum(lax.psum(inner(direction, image, inverse_share), "gx"), "gy")
         step_length = norm_now / curve
         pressure = pressure + step_length * direction
         resid = resid - step_length * image

time: 879 us -> 831 us (0.945)
  blocking collectives: 714 us -> 661 us
    psum x3 -> x6, blocking collectives: 310 us -> 243 us  [the longest x3 139 us: solve_pressure(): lax.psum(inner(direction, image, inverse_share), 'gx')]
    psum x3, blocking collectives: 296 us -> 309 us  [solve_pressure(): norm_next = lax.psum(inner(resid, resid, inverse_share), ('gx', 'gy'))]
where the time goes in v1:
time: 831 us; the launch traced here: 826 us
  blocking collectives  661 us (80%)
  starting transfers between devices  95.9 us (12%)
  waiting for transfers between devices  29.5 us (4%)
  between operations  10.9 us (1%)
  other arithmetic  10 us (1%)
  matrix products  9.55 us (1%)
  local copies, waits for them, and re-layouts  9.23 us (1%)
    psum x3, blocking collectives, solve_pressure(): norm_next = lax.psum(inner(resid, resid, inverse_share), ('gx', 'gy'))  309 us
    psum x3, blocking collectives, solve_pressure(): lax.psum(inner(direction, image, inverse_share), 'gx')  139 us
    psum x1, blocking collectives, solve_pressure(): lax.psum((inner(resid, resid, inverse_share), inner(direction, image, inv...  109 us
    psum x3, blocking collectives, solve_pressure(): lax.psum(lax.psum(inner(direction, image, inverse_share), 'gx'), 'gy')  104 us
    ppermute x14, starting transfers between devices, with_halo(): after = lax.ppermute(initial, axis, down)  60.9 us
    ppermute x14, starting transfers between devices, with_halo(): before = lax.ppermute(last, axis, up)  35 us
    ppermute x14, waiting for transfers between devices, with_halo(): after = lax.ppermute(initial, axis, down)  16.8 us
  transfers between devices with their start and end apart: 28, of which 27 were waited for; matrix products, arithmetic and copies ran while one was open for 0% of the time, Pallas kernels for 0%

profile of v1, /device:TPU:1, one launch (start us, length us, event | category | flops | bytes accessed | tf_op | source)
XLA Modules:
  0.0 825.8 jit_solution(8232312190961975468)
XLA Ops:
  0.7 0.7 copy-done.11
  1.3 1.3 convolution_bitcast_fusion.3
  6.4 0.7 copy-done.13
  9.0 3.0 collective-permute-start
  12.1 3.9 collective-permute-start.1
  17.0 1.9 collective-permute-start.2
  18.9 6.7 collective-permute-start.3
  25.6 2.2 collective-permute-done.2
  27.8 1.5 collective-permute-done.3
  30.0 0.8 copy-done.1
  32.4 1.8 collective-permute-start.4
  34.3 3.5 collective-permute-start.5
  38.7 1.9 collective-permute-start.6
  40.6 7.4 collective-permute-start.7
  48.1 1.6 collective-permute-done.7
  50.9 0.7 copy-done.3
  53.3 6.4 collective-permute-start.9
  60.6 1.9 collective-permute-start.10
  62.6 7.4 collective-permute-start.11
  70.0 1.6 collective-permute-done.11
  71.8 0.8 multiply_reduce_fusion.5
  72.6 108.5 %all-reduce = (f32[]{:T(128)}, f32[]{:T(128)}) all-reduce(f32[]{:T(128)} %get-tuple-element.3, f32[]{:T(128)} %get-tuple-element.2), channel_id=1, replica_groups=mesh['gx'=32,'gy'=16] {'gx','gy'}, use_global_device_ids=true, to_apply=%region_4.5 | all-reduce | flops 2 | bytes 16 | tf_op jit(solution)/shard_map/psum | solution.py:156
  182.5 0.7 multiply_reduce_fusion.4
  183.2 98.5 %psum.79 = f32[]{:T(128)} all-reduce(f32[]{:T(128)} %multiply_reduce_fusion.4), channel_id=1, replica_groups=mesh['gx'=32,'gy'=16] {'gx','gy'}, use_global_device_ids=true, to_apply=%region_8.9 | all-reduce | flops 1 | bytes 8 | tf_op jit(solution)/shard_map/psum | solution.py:166
  284.5 2.3 collective-permute-start.12
  286.8 0.8 collective-permute-done.12
  287.6 2.3 collective-permute-done.13
  289.9 2.2 collective-permute-start.14
  292.2 6.4 collective-permute-start.15
  298.6 1.4 collective-permute-done.14
  299.9 0.9 collective-permute-done.15
  301.1 0.7 multiply_reduce_fusion.3
  301.8 46.5 %psum.80 = f32[]{:T(128)} all-reduce(f32[]{:T(128)} %get-tuple-element.10), channel_id=1, replica_groups=mesh['gx'=32,'gy'=16] {'gx'}, use_global_device_ids=true, to_apply=%region_10.11 | all-reduce | flops 1 | bytes 8 | tf_op jit(solution)/shard_map/psum | solution.py:161
  348.3 34.6 %psum.81 = f32[]{:T(128)} all-reduce(f32[]{:T(128)} %psum.80), channel_id=1, replica_groups=mesh['gx'=32,'gy'=16] {'gy'}, use_global_device_ids=true, to_apply=%region_11.12 | all-reduce | flops 1 | bytes 8 | tf_op jit(solution)/shard_map/psum | solution.py:161
  384.3 0.7 multiply_reduce_fusion.2
  385.0 105.1 %psum.82 = f32[]{:T(128)} all-reduce(f32[]{:T(128)} %get-tuple-element.8), channel_id=1, replica_groups=mesh['gx'=32,'gy'=16] {'gx','gy'}, use_global_device_ids=true, to_apply=%region_13.14 | all-reduce | flops 1 | bytes 8 | tf_op jit(solution)/shard_map/psum | solution.py:166
  492.8 2.3 collective-permute-start.16
  495.1 0.8 collective-permute-done.16
  495.8 2.3 collective-permute-done.17
  498.2 3.2 collective-permute-start.18
  501.5 5.4 collective-permute-start.19
  506.8 1.4 collective-permute-done.18
  508.2 0.9 collective-permute-done.19
  509.4 0.7 multiply_reduce_fusion.1
  510.1 46.5 %psum.83 = f32[]{:T(128)} all-reduce(f32[]{:T(128)} %get-tuple-element.6), channel_id=1, replica_groups=mesh['gx'=32,'gy'=16] {'gx'}, use_global_device_ids=true, to_apply=%region_15.16 | all-reduce | flops 1 | bytes 8 | tf_op jit(solution)/shard_map/psum | solution.py:161
  556.6 34.6 %psum.84 = f32[]{:T(128)} all-reduce(f32[]{:T(128)} %psum.83), channel_id=1, replica_groups=mesh['gx'=32,'gy'=16] {'gy'}, use_global_device_ids=true, to_apply=%region_16.17 | all-reduce | flops 1 | bytes 8 | tf_op jit(solution)/shard_map/psum | solution.py:161
  593.2 105.3 %psum.85 = f32[]{:T(128)} all-reduce(f32[]{:T(128)} %multiply_reduce_fusion), channel_id=1, replica_groups=mesh['gx'=32,'gy'=16] {'gx','gy'}, use_global_device_ids=true, to_apply=%region_18.19 | all-reduce | flops 1 | bytes 8 | tf_op jit(solution)/shard_map/psum | solution.py:166
  701.1 2.3 collective-permute-start.20
  703.4 0.8 collective-permute-done.20
  704.2 2.3 collective-permute-done.21
  706.6 3.2 collective-permute-start.22
  709.8 5.4 collective-permute-start.23
  715.2 1.4 collective-permute-done.22
  716.6 0.9 collective-permute-done.23
  717.7 0.7 fusion.73
  718.5 46.5 %psum.86 = f32[]{:T(128)} all-reduce(f32[]{:T(128)} %fusion.73), channel_id=1, replica_groups=mesh['gx'=32,'gy'=16] {'gx'}, use_global_device_ids=true, to_apply=%region_20.21 | all-reduce | flops 1 | bytes 8 | tf_op jit(solution)/shard_map/psum | solution.py:161
  764.9 34.6 %psum.87 = f32[]{:T(128)} all-reduce(f32[]{:T(128)} %psum.86), channel_id=1, replica_groups=mesh['gx'=32,'gy'=16] {'gy'}, use_global_device_ids=true, to_apply=%region_21.22 | all-reduce | flops 1 | bytes 8 | tf_op jit(solution)/shard_map/psum | solution.py:161
  801.9 6.8 collective-permute-start.24
  808.8 1.9 collective-permute-start.25
  812.1 1.9 collective-permute-start.26
  814.0 6.7 collective-permute-start.27
  820.7 2.2 collective-permute-done.26
  822.9 1.5 collective-permute-done.27
  824.9 1.0 fusion.35
  (162 shorter events, 22.6 us)
Async XLA Ops:
  0.6 0.7 copy-start.11
  1.3 1.3 copy-start
  1.3 1.3 copy-start.2
  2.7 0.8 copy-start.6
  4.1 0.7 copy-start.15
  4.9 0.7 copy-start.12
  6.4 0.7 copy-start.13
  7.1 0.7 copy-start.14
  7.7 0.8 copy-start.10
  9.0 7.6 collective-permute-start
  12.1 3.9 copy-start.16
  12.1 4.7 collective-permute-start.1
  17.0 10.8 %collective-permute-start.2 = (f32[3,8,18,1]{3,2,1,0:T(8,128)S(1)}, f32[3,8,18,1]{3,2,1,0:T(8,128)S(1)}, u32[]{:S(2)}, u32[]{:S(2)}) collective-permute-start(f32[3,8,18,1]{3,2,1,0:T(8,128)S(1)} %get-tuple-element.15), channel_id=1, source_target_pairs={{0,1},{1,2},{2,3},{3,4},{4,5},{5,6},{6,7},{7,8},{8,9},{9,10},{10,1... | collective-permute-start | bytes 5192 | tf_op jit(solution)/shard_map/ppermute | solution.py:44
  18.9 10.3 %collective-permute-start.3 = (f32[3,8,18,1]{3,2,1,0:T(8,128)S(1)}, f32[3,8,18,1]{3,2,1,0:T(8,128)S(1)}, u32[]{:S(2)}, u32[]{:S(2)}) collective-permute-start(f32[3,8,18,1]{3,2,1,0:T(8,128)S(1)} %get-tuple-element.16), channel_id=1, source_target_pairs={{1,0},{2,1},{3,2},{4,3},{5,4},{6,5},{7,6},{8,7},{9,8},{10,9},{11,1... | collective-permute-start | bytes 5192 | tf_op jit(solution)/shard_map/ppermute | solution.py:45
  30.0 0.8 copy-start.1
  30.8 0.7 copy-start.7
  31.5 0.7 copy-start.5
  32.4 5.9 collective-permute-start.4
  34.3 4.3 collective-permute-start.5
  38.7 9.4 %collective-permute-start.6 = (f32[1,8,18,1]{3,2,1,0:T(8,128)S(1)}, f32[1,8,18,1]{3,2,1,0:T(8,128)S(1)}, u32[]{:S(2)}, u32[]{:S(2)}) collective-permute-start(f32[1,8,18,1]{3,2,1,0:T(8,128)S(1)} %get-tuple-element.32), channel_id=1, source_target_pairs={{0,1},{1,2},{2,3},{3,4},{4,5},{5,6},{6,7},{7,8},{8,9},{9,10},{10,1... | collective-permute-start | bytes 1736 | tf_op jit(solution)/shard_map/ppermute | solution.py:44
  40.6 9.1 %collective-permute-start.7 = (f32[1,8,18,1]{3,2,1,0:T(8,128)S(1)}, f32[1,8,18,1]{3,2,1,0:T(8,128)S(1)}, u32[]{:S(2)}, u32[]{:S(2)}) collective-permute-start(f32[1,8,18,1]{3,2,1,0:T(8,128)S(1)} %get-tuple-element.33), channel_id=1, source_target_pairs={{1,0},{2,1},{3,2},{4,3},{5,4},{6,5},{7,6},{8,7},{9,8},{10,9},{11,1... | collective-permute-start | bytes 1736 | tf_op jit(solution)/shard_map/ppermute | solution.py:45
  50.8 0.8 copy-start.3
  51.6 0.7 copy-start.9
  52.3 0.7 copy-start.8
  53.3 7.1 collective-permute-start.8
  53.3 7.3 collective-permute-start.9
  60.6 9.4 %collective-permute-start.10 = (f32[1,8,18,1]{3,2,1,0:T(8,128)S(1)}, f32[1,8,18,1]{3,2,1,0:T(8,128)S(1)}, u32[]{:S(2)}, u32[]{:S(2)}) collective-permute-start(f32[1,8,18,1]{3,2,1,0:T(8,128)S(1)} %get-tuple-element.30), channel_id=1, source_target_pairs={{0,1},{1,2},{2,3},{3,4},{4,5},{5,6},{6,7},{7,8},{8,9},{9,10},{10,1... | collective-permute-start | bytes 1736 | tf_op jit(solution)/shard_map/ppermute | solution.py:44
  62.6 9.0 %collective-permute-start.11 = (f32[1,8,18,1]{3,2,1,0:T(8,128)S(1)}, f32[1,8,18,1]{3,2,1,0:T(8,128)S(1)}, u32[]{:S(2)}, u32[]{:S(2)}) collective-permute-start(f32[1,8,18,1]{3,2,1,0:T(8,128)S(1)} %get-tuple-element.31), channel_id=1, source_target_pairs={{1,0},{2,1},{3,2},{4,3},{5,4},{6,5},{7,6},{8,7},{9,8},{10,9},{11,1... | collective-permute-start | bytes 1736 | tf_op jit(solution)/shard_map/ppermute | solution.py:45
  284.5 3.1 collective-permute-start.12
  286.8 3.0 collective-permute-start.13
  289.9 10.0 %collective-permute-start.14 = (f32[1,8,18,1]{3,2,1,0:T(8,128)S(1)}, f32[1,8,18,1]{3,2,1,0:T(8,128)S(1)}, u32[]{:S(2)}, u32[]{:S(2)}) collective-permute-start(f32[1,8,18,1]{3,2,1,0:T(8,128)S(1)} %get-tuple-element.28), channel_id=1, source_target_pairs={{0,1},{1,2},{2,3},{3,4},{4,5},{5,6},{6,7},{7,8},{8,9},{9,10},{10,1... | collective-permute-start | bytes 1736 | tf_op jit(solution)/shard_map/ppermute | solution.py:44
  292.2 8.7 %collective-permute-start.15 = (f32[1,8,18,1]{3,2,1,0:T(8,128)S(1)}, f32[1,8,18,1]{3,2,1,0:T(8,128)S(1)}, u32[]{:S(2)}, u32[]{:S(2)}) collective-permute-start(f32[1,8,18,1]{3,2,1,0:T(8,128)S(1)} %get-tuple-element.29), channel_id=1, source_target_pairs={{1,0},{2,1},{3,2},{4,3},{5,4},{6,5},{7,6},{8,7},{9,8},{10,9},{11,1... | collective-permute-start | bytes 1736 | tf_op jit(solution)/shard_map/ppermute | solution.py:45
  492.8 3.0 collective-permute-start.16
  495.1 3.0 collective-permute-start.17
  498.2 10.0 %collective-permute-start.18 = (f32[1,8,18,1]{3,2,1,0:T(8,128)S(1)}, f32[1,8,18,1]{3,2,1,0:T(8,128)S(1)}, u32[]{:S(2)}, u32[]{:S(2)}) collective-permute-start(f32[1,8,18,1]{3,2,1,0:T(8,128)S(1)} %get-tuple-element.26), channel_id=1, source_target_pairs={{0,1},{1,2},{2,3},{3,4},{4,5},{5,6},{6,7},{7,8},{8,9},{9,10},{10,1... | collective-permute-start | bytes 1736 | tf_op jit(solution)/shard_map/ppermute | solution.py:44
  501.5 7.6 collective-permute-start.19
  701.1 3.0 collective-permute-start.20
  703.4 3.0 collective-permute-start.21
  706.6 10.0 %collective-permute-start.22 = (f32[1,8,18,1]{3,2,1,0:T(8,128)S(1)}, f32[1,8,18,1]{3,2,1,0:T(8,128)S(1)}, u32[]{:S(2)}, u32[]{:S(2)}) collective-permute-start(f32[1,8,18,1]{3,2,1,0:T(8,128)S(1)} %get-tuple-element.24), channel_id=1, source_target_pairs={{0,1},{1,2},{2,3},{3,4},{4,5},{5,6},{6,7},{7,8},{8,9},{9,10},{10,1... | collective-permute-start | bytes 1736 | tf_op jit(solution)/shard_map/ppermute | solution.py:44
  709.8 7.6 collective-permute-start.23
  801.0 0.6 copy-start.4
  801.9 9.3 %collective-permute-start.24 = (f32[3,8,1,128]{3,2,1,0:T(1,128)S(1)}, f32[3,8,1,128]{3,2,1,0:T(1,128)S(1)}, u32[]{:S(2)}, u32[]{:S(2)}) collective-permute-start(f32[3,8,1,128]{3,2,1,0:T(1,128)S(1)} %get-tuple-element.17), channel_id=1, source_target_pairs={{0,16},{16,32},{32,48},{48,64},{64,80},{80,96},{96,112},{112,128},... | collective-permute-start | bytes 36872 | tf_op jit(solution)/shard_map/ppermute | solution.py:44
  808.8 3.1 collective-permute-start.25
  812.1 10.8 %collective-permute-start.26 = (f32[3,8,18,1]{3,2,1,0:T(8,128)S(1)}, f32[3,8,18,1]{3,2,1,0:T(8,128)S(1)}, u32[]{:S(2)}, u32[]{:S(2)}) collective-permute-start(f32[3,8,18,1]{3,2,1,0:T(8,128)S(1)} %get-tuple-element.13), channel_id=1, source_target_pairs={{0,1},{1,2},{2,3},{3,4},{4,5},{5,6},{6,7},{7,8},{8,9},{9,10},{10,1... | collective-permute-start | bytes 5192 | tf_op jit(solution)/shard_map/ppermute | solution.py:44
  814.0 10.3 %collective-permute-start.27 = (f32[3,8,18,1]{3,2,1,0:T(8,128)S(1)}, f32[3,8,18,1]{3,2,1,0:T(8,128)S(1)}, u32[]{:S(2)}, u32[]{:S(2)}) collective-permute-start(f32[3,8,18,1]{3,2,1,0:T(8,128)S(1)} %get-tuple-element.14), channel_id=1, source_target_pairs={{1,0},{2,1},{3,2},{4,3},{5,4},{6,5},{7,6},{8,7},{9,8},{10,9},{11,1... | collective-permute-start | bytes 5192 | tf_op jit(solution)/shard_map/ppermute | solution.py:45
